TPU v7x, 1024 devices: a whole 8x8x8 slice. The times are simulated.
1024 devices in a mesh: comp: 32 (over z, x_lo), tile: 32 (over x_hi, y, core).
Axes of the slice: x: 8 (x_hi: 2, x_lo: 4; x = x_hi * 4 + x_lo), y: 8, z: 8, core: 2. Of those that a mesh axis runs over, the one named last changes fastest.
Arguments:
- tracers: float32 [2, 72, 256, 4096], P(None, None, 'tile', 'comp'), may hold values from -8 to 8
- surface_fields: float32 [4, 256, 4096], P(None, 'tile', 'comp'), may hold values from -6 to 6
- lateral_rate: bfloat16 [256, 4096], P('tile', 'comp'), may hold values from 0.0099487305 to 0.19921875
- vertical_rate: bfloat16 [71, 256, 4096], P(None, 'tile', 'comp'), may hold values from 0.0029907227 to 0.25
- coupling_gain: float32 [32, 2, 4], P('comp'), may hold values from -4 to 4
- send_slots: int32 [32, 32, 32, 2], P('comp', None, 'tile'), may hold values from -1 to 7, as said below
- recv_slots: int32 [32, 32, 32, 2], P('comp', None, 'tile'), may hold values from -1 to 7, as said below
- remap_weights: bfloat16 [32, 32, 32, 2, 128, 128], P('comp', None, 'tile'), may hold values from -0.5 to 0.5
Outputs:
- tracers_next: float32 [2, 72, 256, 4096], P(None, None, 'tile', 'comp')
Inputs may be any that keep to these rules, and one draw needn't show every extreme that they name: `send_slots`: -1 marks an empty slot, else a block of the sender. Slots are live only between an atmosphere row and an ocean row, each such pair of devices having 1 to 2 live slots, live ones first; most such pairs fill all 2, in every tile and from every receiver's view too. recv_slots[q, r, t, s] is live exactly where send_slots[r, q, t, s] is, and then names a block of the receiver; -1 elsewhere.
All inputs are finite; a program needn't handle non-finite values.
Results may differ from a plain program's by a relative error of at most 0.00045.
Values sent between devices are 32-bit elements; how exact they have to be, the bound alone decides.
A program may use at most 32 MiB of HBM per device.

v0:
```python
import jax
import jax.numpy as jnp
from jax import lax
from jax.sharding import PartitionSpec as P

OLEV = 60
STEPS = 2


def with_halo(block, sides, width):
    for axis, dim in sides:
        count = lax.axis_size(axis)
        forward = [(i, i + 1) for i in range(count - 1)]
        forward.append((count - 1, 0))
        backward = [(target, source) for source, target in forward]
        low = lax.ppermute(
            lax.slice_in_dim(block, block.shape[dim] - width, None, axis=dim), axis, forward
        )
        high = lax.ppermute(lax.slice_in_dim(block, 0, width, axis=dim), axis, backward)
        block = jnp.concatenate([low, block, high], axis=dim)
    return block


def advance(extended, lateral, vertical, forcing, active):
    centre = extended[:, :, 1:-1, 1:-1]
    laplace = (
        extended[:, :, 2:, 1:-1]
        + extended[:, :, :-2, 1:-1]
        + extended[:, :, 1:-1, 2:]
        + extended[:, :, 1:-1, :-2]
        - 4.0 * centre
    )
    coupled = vertical * active[1:].astype(jnp.float32)
    flux_down = coupled * (centre[:, 1:] - centre[:, :-1])
    zero_level = jnp.zeros_like(flux_down[:, :1])
    mixing = jnp.concatenate([flux_down, zero_level], 1) - jnp.concatenate(
        [zero_level, flux_down], 1
    )
    updated = centre + lateral * laplace + mixing
    updated = updated.at[:, 0].add(forcing)
    return jnp.where(active, updated, centre)


def mirror_edges(extended, margin, lower_wall, upper_wall):
    lower = jnp.flip(extended[..., margin : 2 * margin], -1)
    upper = jnp.flip(extended[..., -2 * margin : -margin], -1)
    return jnp.concatenate(
        [
            jnp.where(lower_wall, lower, extended[..., :margin]),
            extended[..., margin:-margin],
            jnp.where(upper_wall, upper, extended[..., -margin:]),
        ],
        -1,
    )


def per_device(
    tracers,
    surface_fields,
    lateral_rate,
    vertical_rate,
    coupling_gain,
    send_slots,
    recv_slots,
    remap_weights,
):
    highest = lax.Precision.HIGHEST
    rows_total = lax.axis_size("comp")
    row_here = lax.axis_index("comp")
    atmos_rows = 3 * rows_total // 4
    blocks_x = tracers.shape[2]
    levels = tracers.shape[1]
    is_ocean = row_here >= atmos_rows
    active = jnp.logical_or(jnp.logical_not(is_ocean), jnp.arange(levels) < OLEV)[:, None, None]
    lower_wall = jnp.logical_or(row_here == 0, row_here == atmos_rows)
    upper_wall = jnp.logical_or(row_here == atmos_rows - 1, row_here == rows_total - 1)
    chosen = send_slots[0, :, 0]
    by_block = jnp.moveaxis(surface_fields, 1, 0)
    outgoing = by_block[jnp.clip(chosen, 0, blocks_x - 1)]
    outgoing = jnp.where((chosen >= 0)[:, :, None, None], outgoing, 0.0)
    weights = remap_weights[0, :, 0]
    landing = (recv_slots[0, :, 0][..., None] == jnp.arange(blocks_x)).astype(jnp.float32)
    contrib = jnp.einsum(
        "rsfi,rsij->rsfj",
        lax.all_to_all(outgoing, "comp", split_axis=0, concat_axis=0, tiled=True),
        weights.astype(jnp.float32),
        precision=highest,
    )
    remapped = jnp.einsum("rsx,rsfj->fxj", landing, contrib, precision=highest)
    forcing = jnp.einsum("vf,fxy->vxy", coupling_gain[0], remapped, precision=highest)
    lateral = lateral_rate.astype(jnp.float32)
    vertical = vertical_rate.astype(jnp.float32)
    current = tracers
    for repeat in range(STEPS):
        extended = with_halo(current, (("comp", 3), ("tile", 2)), 1)
        extended = mirror_edges(extended, 1, lower_wall, upper_wall)
        current = advance(extended, lateral, vertical, forcing, active)
    return current


def solution(mesh):
    return jax.shard_map(
        per_device,
        mesh=mesh,
        in_specs=(
            P(None, None, "tile", "comp"),
            P(None, "tile", "comp"),
            P("tile", "comp"),
            P(None, "tile", "comp"),
            P("comp", None, None),
            P("comp", None, "tile", None),
            P("comp", None, "tile", None),
            P("comp", None, "tile", None, None, None),
        ),
        out_specs=P(None, None, "tile", "comp"),
        check_vma=False,
    )
```

profile of v0, /device:TPU:14, one launch (start us, length us, event | category | flops | bytes accessed | tf_op | source)
XLA Modules:
  0.0 120.3 jit_solution(12272399325771144328)
XLA Ops:
  0.0 2.4 %fusion.27 = (f32[2,72,8,1]{3,2,1,0:T(8,128)}, f32[2,72,8,1]{3,2,1,0:T(8,128)S(1)}) fusion(f32[2,72,8,128]{3,2,1,0:T(8,128)} %param.12), kind=kLoop, calls=%fused_computation.72 | loop fusion | bytes 18432 | tf_op jit(solution)/shard_map/slice | solution.py:17
  2.4 2.0 %copy.55 = f32[2,72,8,1]{1,2,3,0:T(8,128)} copy(f32[2,72,8,1]{3,2,1,0:T(8,128)} %get-tuple-element.39) | data formatting | bytes 9216
  4.4 7.8 %collective-permute-start = (f32[2,72,8,1]{1,2,3,0:T(8,128)}, f32[2,72,8,1]{1,2,3,0:T(8,128)}, u32[]{:S(2)}, u32[]{:S(2)}) collective-permute-start(f32[2,72,8,1]{1,2,3,0:T(8,128)} %copy.55), channel_id=1, source_target_pairs={{0,32},{32,64},{64,96},{96,128},{128,160},{160,192},{192,224},{224... | collective-permute-start | bytes 13832 | tf_op jit(solution)/shard_map/ppermute | solution.py:16
  13.0 1.9 %collective-permute-start.1 = (f32[2,72,8,1]{1,2,3,0:T(8,128)}, f32[2,72,8,1]{1,2,3,0:T(8,128)}, u32[]{:S(2)}, u32[]{:S(2)}) collective-permute-start(f32[2,72,8,1]{1,2,3,0:T(8,128)} %copy.56), channel_id=1, source_target_pairs={{32,0},{64,32},{96,64},{128,96},{160,128},{192,160},{224,192},{256... | collective-permute-start | bytes 13832 | tf_op jit(solution)/shard_map/ppermute | solution.py:19
  16.8 18.8 %all-to-all-start = ((f32[32,2,4,128]{3,2,1,0:T(4,128)}), f32[32,2,4,128]{3,2,1,0:T(4,128)S(1)}, u32[]{:S(2)}, u32[]{:S(2)}) async-start(f32[32,2,4,128]{3,2,1,0:T(4,128)} %broadcast_select_fusion.2), calls=%async_computation | async-start | bytes 262144 | tf_op jit(solution)/shard_map/all_to_all | solution.py:85
  38.7 1.8 %copy.38 = f32[2,72,8,1]{3,0,2,1:T(2,128)} copy(f32[2,72,8,1]{1,2,3,0:T(8,128)} %collective-permute-done.1) | data formatting | bytes 9216 | tf_op jit(solution)/shard_map/ppermute | solution.py:19
  40.6 2.2 %pad_maximum_fusion.21 = (f32[2,72,1,130]{3,0,2,1:T(2,128)}, f32[2,72,1,130]{3,0,2,1:T(2,128)}) fusion(f32[2,72,8,1]{3,0,2,1:T(2,128)} %copy.38, f32[2,72,8,128]{3,0,2,1:T(2,128)S(1)} %copy.40, f32[2,72,8,1]{3,0,2,1:T(2,128)S(1)} %copy.36), kind=kLoop, calls=%fused_computation.51 | loop fusion | flops 74880 | bytes 748800 | tf_op jit(solution)/shard_map/concatenate | solution.py:20
  42.8 5.1 %collective-permute-start.2 = (f32[2,72,1,130]{3,0,2,1:T(2,128)}, f32[2,72,1,130]{3,0,2,1:T(2,128)S(1)}, u32[]{:S(2)}, u32[]{:S(2)}) collective-permute-start(f32[2,72,1,130]{3,0,2,1:T(2,128)} %get-tuple-element.32), channel_id=1, source_target_pairs={{1,0},{2,1},{3,2},{4,3},{5,4},{6,5},{7,6},{8,7},{9,8},{10,9},{11,1... | collective-permute-start | bytes 224648 | tf_op jit(solution)/shard_map/ppermute | solution.py:19
  47.8 2.1 %collective-permute-start.3 = (f32[2,72,1,130]{3,0,2,1:T(2,128)}, f32[2,72,1,130]{3,0,2,1:T(2,128)}, u32[]{:S(2)}, u32[]{:S(2)}) collective-permute-start(f32[2,72,1,130]{3,0,2,1:T(2,128)} %get-tuple-element.31), channel_id=1, source_target_pairs={{0,1},{1,2},{2,3},{3,4},{4,5},{5,6},{6,7},{7,8},{8,9},{9,10},{10,1... | collective-permute-start | bytes 224648 | tf_op jit(solution)/shard_map/ppermute | solution.py:16
  52.4 8.3 %collective-permute-done.3 = f32[2,72,1,130]{3,0,2,1:T(2,128)} collective-permute-done((f32[2,72,1,130]{3,0,2,1:T(2,128)}, f32[2,72,1,130]{3,0,2,1:T(2,128)}, u32[]{:S(2)}, u32[]{:S(2)}) %collective-permute-start.3) | collective-permute-done | bytes 74912 | tf_op jit(solution)/shard_map/ppermute | solution.py:16
  60.6 3.4 %pad_maximum_fusion = f32[2,72,10,130]{3,0,2,1:T(2,128)S(1)} fusion(f32[2,72,1,130]{3,0,2,1:T(2,128)S(1)} %collective-permute-done.2, f32[2,72,8,1]{3,0,2,1:T(2,128)} %copy.38, f32[2,72,8,128]{3,0,2,1:T(2,128)S(1)} %copy.40, f32[2,72,8,1]{3,0,2,1:T(2,128)S(1)} %copy.36, f32[2,72,1,130]{3,0,2,1:T(2,128)} %collective-permute-done.3), kind=kLoop, calls=%fused_computation.3 | loop fusion | flops 748800 | bytes 1497600 | tf_op jit(solution)/shard_map/concatenate | solution.py:20
  64.9 1.6 %slice_select_fusion.3 = (f32[2,72,10,1]{3,0,2,1:T(2,128)S(1)}, f32[2,72,10,1]{3,0,2,1:T(2,128)S(1)}) fusion(f32[2,72,10,130]{3,0,2,1:T(2,128)S(1)} %pad_maximum_fusion, pred[]{:T(512)S(6)} %or.14, pred[]{:T(512)S(6)} %or.15), kind=kLoop, calls=%fused_computation.10 | loop fusion | flops 2880 | bytes 34562 | tf_op jit(solution)/shard_map/jit(_where)/select_n | solution.py:51
  66.5 5.2 %fusion.13 = f32[2,72,8,128]{3,0,2,1:T(2,128)} fusion(f32[2,72,8,128]{3,0,2,1:T(2,128)S(1)} %copy.40, f32[2,72,10,128]{3,0,2,1:T(2,128)S(1)} %slice.202, f32[2,72,10,1]{3,0,2,1:T(2,128)S(1)} %get-tuple-element.36, f32[2,72,10,1]{3,0,2,1:T(2,128)S(1)} %get-tuple-element.35, f32[2,72,1,130]{3,0,2,1:T(2,128)} %collective-permute-done.3, ...), kind=kLoop, calls=%fused_computation.31 | loop fusion | flops 2506752 | bytes 2673152 | tf_op jit(solution)/shard_map/add | solution.py:39
  71.7 1.7 %fusion = f32[32,2,4,128]{3,2,1,0:T(4,128)S(1)} fusion(f32[32,2,4,128]{3,2,1,0:T(4,128)S(1)} %all-to-all-done, bf16[1,32,1,2,128,128]{5,4,3,2,1,0:T(8,128)(2,1)S(1)} %copy-done), kind=kOutput, calls=%fused_computation.1 | convolution fusion | flops 50331648 | bytes 2359296 | tf_op jit(solution)/shard_map/rsfi,rsij->rsfj/dot_general | solution.py:83
  75.1 1.7 %broadcast_select_fusion.1 = f32[2,72,8,128]{3,0,2,1:T(2,128)S(1)} fusion(f32[2,72,8,128]{3,0,2,1:T(2,128)} %get-tuple-element.41, pred[72]{0:T(512)(128)(4,1)S(1)} %copy-done.13, f32[2,72,8,128]{3,2,1,0:T(8,128)S(1)} %copy-done.4), kind=kLoop, calls=%fused_computation.42 | loop fusion | flops 147456 | bytes 1769544 | tf_op jit(solution)/shard_map/jit(_where)/select_n | solution.py:41
  79.7 3.5 %collective-permute-start.4 = (f32[2,72,8,1]{1,2,3,0:T(8,128)S(1)}, f32[2,72,8,1]{1,2,3,0:T(8,128)S(1)}, u32[]{:S(2)}, u32[]{:S(2)}) collective-permute-start(f32[2,72,8,1]{1,2,3,0:T(8,128)S(1)} %copy.49), channel_id=1, source_target_pairs={{0,32},{32,64},{64,96},{96,128},{128,160},{160,192},{192,224},{224... | collective-permute-start | bytes 13832 | tf_op jit(solution)/shard_map/ppermute | solution.py:16
  83.5 2.5 %collective-permute-start.5 = (f32[2,72,8,1]{1,2,3,0:T(8,128)S(1)}, f32[2,72,8,1]{1,2,3,0:T(8,128)S(1)}, u32[]{:S(2)}, u32[]{:S(2)}) collective-permute-start(f32[2,72,8,1]{1,2,3,0:T(8,128)S(1)} %copy.50), channel_id=1, source_target_pairs={{32,0},{64,32},{96,64},{128,96},{160,128},{192,160},{224,192},{256... | collective-permute-start | bytes 13832 | tf_op jit(solution)/shard_map/ppermute | solution.py:19
  86.5 5.2 %collective-permute-done.5 = f32[2,72,8,1]{1,2,3,0:T(8,128)S(1)} collective-permute-done((f32[2,72,8,1]{1,2,3,0:T(8,128)S(1)}, f32[2,72,8,1]{1,2,3,0:T(8,128)S(1)}, u32[]{:S(2)}, u32[]{:S(2)}) %collective-permute-start.5) | collective-permute-done | bytes 4640 | tf_op jit(solution)/shard_map/ppermute | solution.py:19
  94.3 2.1 %collective-permute-start.6 = (f32[2,72,1,130]{3,0,2,1:T(2,128)S(1)}, f32[2,72,1,130]{3,0,2,1:T(2,128)S(1)}, u32[]{:S(2)}, u32[]{:S(2)}) collective-permute-start(f32[2,72,1,130]{3,0,2,1:T(2,128)S(1)} %get-tuple-element.30), channel_id=1, source_target_pairs={{1,0},{2,1},{3,2},{4,3},{5,4},{6,5},{7,6},{8,7},{9,8},{10,9},{11,1... | collective-permute-start | bytes 224648 | tf_op jit(solution)/shard_map/ppermute | solution.py:19
  96.4 2.6 %collective-permute-start.7 = (f32[2,72,1,130]{3,0,2,1:T(2,128)S(1)}, f32[2,72,1,130]{3,0,2,1:T(2,128)S(1)}, u32[]{:S(2)}, u32[]{:S(2)}) collective-permute-start(f32[2,72,1,130]{3,0,2,1:T(2,128)S(1)} %get-tuple-element.29), channel_id=1, source_target_pairs={{0,1},{1,2},{2,3},{3,4},{4,5},{5,6},{6,7},{7,8},{8,9},{9,10},{10,1... | collective-permute-start | bytes 224648 | tf_op jit(solution)/shard_map/ppermute | solution.py:16
  100.7 9.8 %collective-permute-done.7 = f32[2,72,1,130]{3,0,2,1:T(2,128)S(1)} collective-permute-done((f32[2,72,1,130]{3,0,2,1:T(2,128)S(1)}, f32[2,72,1,130]{3,0,2,1:T(2,128)S(1)}, u32[]{:S(2)}, u32[]{:S(2)}) %collective-permute-start.7) | collective-permute-done | bytes 74912 | tf_op jit(solution)/shard_map/ppermute | solution.py:16
  110.5 2.4 %pad_maximum_fusion.1 = f32[2,72,10,130]{3,0,2,1:T(2,128)S(1)} fusion(f32[2,72,1,130]{3,0,2,1:T(2,128)S(1)} %collective-permute-done.6, f32[2,72,8,1]{3,0,2,1:T(2,128)S(1)} %copy-done.2, f32[2,72,8,128]{3,0,2,1:T(2,128)S(1)} %broadcast_select_fusion.1, f32[2,72,8,1]{3,0,2,1:T(2,128)S(1)} %copy.51, f32[2,72,1,130]{3,0,2,1:T(2,128)S(1)} %collective-permute-done.7), kind=kLoop, calls=%fused_computation.4 | loop fusion | flops 748800 | bytes 1497600 | tf_op jit(solution)/shard_map/concatenate | solution.py:20
  112.9 1.6 %slice_select_fusion.1 = (f32[2,72,10,1]{3,0,2,1:T(2,128)S(1)}, f32[2,72,10,1]{3,0,2,1:T(2,128)S(1)}) fusion(f32[2,72,10,130]{3,0,2,1:T(2,128)S(1)} %pad_maximum_fusion.1, pred[]{:T(512)S(6)} %or.14, pred[]{:T(512)S(6)} %or.15), kind=kLoop, calls=%fused_computation.8 | loop fusion | flops 2880 | bytes 34562 | tf_op jit(solution)/shard_map/jit(_where)/select_n | solution.py:51
  115.3 3.7 %fusion.6 = f32[2,72,8,128]{3,0,2,1:T(2,128)S(1)} fusion(f32[2,72,8,128]{3,0,2,1:T(2,128)S(1)} %broadcast_select_fusion.1, f32[2,72,10,128]{3,0,2,1:T(2,128)S(1)} %slice.212, f32[2,72,10,1]{3,0,2,1:T(2,128)S(1)} %get-tuple-element.34, f32[2,72,10,1]{3,0,2,1:T(2,128)S(1)} %get-tuple-element.33, f32[2,72,1,130]{3,0,2,1:T(2,128)S(1)} %collective-permute-done.7, ...), kind=kLoop, calls=%fused_computation.16 | loop fusion | flops 2506752 | bytes 2673152 | tf_op jit(solution)/shard_map/add | solution.py:39
  (71 shorter events, 20.6 us)
Async XLA Ops:
  0.0 71.7 %copy-start = (bf16[1,32,1,2,128,128]{5,4,3,2,1,0:T(8,128)(2,1)S(1)}, bf16[1,32,1,2,128,128]{5,4,3,2,1,0:T(8,128)(2,1)}, u32[]{:S(2)}) copy-start(bf16[1,32,1,2,128,128]{5,4,3,2,1,0:T(8,128)(2,1)} %param.19) | copy-start | bytes 6291460
  0.0 15.0 %copy-start.15 = (s32[1,32,1,2]{1,3,2,0:T(2,128)S(1)}, s32[1,32,1,2]{1,3,2,0:T(2,128)}, u32[]{:S(2)}) copy-start(s32[1,32,1,2]{1,3,2,0:T(2,128)} %param.17) | copy-start | bytes 772
  0.0 15.2 %copy-start.11 = (f32[4,8,128]{2,1,0:T(8,128)S(1)}, f32[4,8,128]{2,1,0:T(8,128)}, u32[]{:S(2)}) copy-start(f32[4,8,128]{2,1,0:T(8,128)} %param.13) | copy-start | bytes 49156
  2.4 33.8 %copy-start.8 = (bf16[71,8,128]{2,1,0:T(8,128)(2,1)S(1)}, bf16[71,8,128]{2,1,0:T(8,128)(2,1)}, u32[]{:S(2)}) copy-start(bf16[71,8,128]{2,1,0:T(8,128)(2,1)} %param.15) | copy-start | bytes 436228
  2.4 34.6 %copy-start.3 = (f32[2,72,8,128]{3,2,1,0:T(8,128)S(1)}, f32[2,72,8,128]{3,2,1,0:T(8,128)}, u32[]{:S(2)}) copy-start(f32[2,72,8,128]{3,2,1,0:T(8,128)} %param.12) | copy-start | bytes 1769476
  4.4 33.1 %collective-permute-start = (f32[2,72,8,1]{1,2,3,0:T(8,128)}, f32[2,72,8,1]{1,2,3,0:T(8,128)}, u32[]{:S(2)}, u32[]{:S(2)}) collective-permute-start(f32[2,72,8,1]{1,2,3,0:T(8,128)} %copy.55), channel_id=1, source_target_pairs={{0,32},{32,64},{64,96},{96,128},{128,160},{160,192},{192,224},{224... | collective-permute-start | bytes 13832 | tf_op jit(solution)/shard_map/ppermute | solution.py:16
  13.0 25.7 %collective-permute-start.1 = (f32[2,72,8,1]{1,2,3,0:T(8,128)}, f32[2,72,8,1]{1,2,3,0:T(8,128)}, u32[]{:S(2)}, u32[]{:S(2)}) collective-permute-start(f32[2,72,8,1]{1,2,3,0:T(8,128)} %copy.56), channel_id=1, source_target_pairs={{32,0},{64,32},{96,64},{128,96},{160,128},{192,160},{224,192},{256... | collective-permute-start | bytes 13832 | tf_op jit(solution)/shard_map/ppermute | solution.py:19
  16.8 54.9 %all-to-all-start = ((f32[32,2,4,128]{3,2,1,0:T(4,128)}), f32[32,2,4,128]{3,2,1,0:T(4,128)S(1)}, u32[]{:S(2)}, u32[]{:S(2)}) async-start(f32[32,2,4,128]{3,2,1,0:T(4,128)} %broadcast_select_fusion.2), calls=%async_computation | async-start | bytes 262144 | tf_op jit(solution)/shard_map/all_to_all | solution.py:85
  40.6 9.4 %copy-start.5 = (f32[71,8,128]{2,1,0:T(8,128)S(1)}, f32[71,8,128]{2,1,0:T(8,128)}, u32[]{:S(2)}) copy-start(f32[71,8,128]{2,1,0:T(8,128)} %convert_multiply_fusion) | copy-start | bytes 872452
  42.8 9.6 %collective-permute-start.2 = (f32[2,72,1,130]{3,0,2,1:T(2,128)}, f32[2,72,1,130]{3,0,2,1:T(2,128)S(1)}, u32[]{:S(2)}, u32[]{:S(2)}) collective-permute-start(f32[2,72,1,130]{3,0,2,1:T(2,128)} %get-tuple-element.32), channel_id=1, source_target_pairs={{1,0},{2,1},{3,2},{4,3},{5,4},{6,5},{7,6},{8,7},{9,8},{10,9},{11,1... | collective-permute-start | bytes 224648 | tf_op jit(solution)/shard_map/ppermute | solution.py:19
  47.8 12.8 %collective-permute-start.3 = (f32[2,72,1,130]{3,0,2,1:T(2,128)}, f32[2,72,1,130]{3,0,2,1:T(2,128)}, u32[]{:S(2)}, u32[]{:S(2)}) collective-permute-start(f32[2,72,1,130]{3,0,2,1:T(2,128)} %get-tuple-element.31), channel_id=1, source_target_pairs={{0,1},{1,2},{2,3},{3,4},{4,5},{5,6},{6,7},{7,8},{8,9},{9,10},{10,1... | collective-permute-start | bytes 224648 | tf_op jit(solution)/shard_map/ppermute | solution.py:16
  64.9 1.6 %copy-start.1 = (f32[2,72,8,1]{3,0,2,1:T(2,128)S(1)}, f32[2,72,8,1]{3,0,2,1:T(2,128)}, u32[]{:S(2)}) copy-start(f32[2,72,8,1]{3,0,2,1:T(2,128)} %copy.38) | copy-start | bytes 13828
  64.9 1.6 %copy-start.7 = (f32[2,71,8,128]{3,0,2,1:T(2,128)S(1)}, f32[2,71,8,128]{3,0,2,1:T(2,128)}, u32[]{:S(2)}) copy-start(f32[2,71,8,128]{3,0,2,1:T(2,128)} %fusion.17) | copy-start | bytes 1744900
  64.9 1.6 %copy-start.9 = (f32[8,128]{1,0:T(8,128)S(1)}, f32[8,128]{1,0:T(8,128)}, u32[]{:S(2)}) copy-start(f32[8,128]{1,0:T(8,128)} %convert_element_type.13) | copy-start | bytes 12292
  71.7 1.8 %copy-start.14 = (s32[1,32,1,2]{1,3,2,0:T(2,128)S(1)}, s32[1,32,1,2]{1,3,2,0:T(2,128)}, u32[]{:S(2)}) copy-start(s32[1,32,1,2]{1,3,2,0:T(2,128)} %param.18) | copy-start | bytes 772
  71.7 2.0 %copy-start.16 = (f32[1,2,4]{2,1,0:T(2,128)S(1)}, f32[1,2,4]{2,1,0:T(2,128)}, u32[]{:S(2)}) copy-start(f32[1,2,4]{2,1,0:T(2,128)} %param.16) | copy-start | bytes 100
  71.7 3.4 %copy-start.4 = (f32[2,72,8,128]{3,2,1,0:T(8,128)S(1)}, f32[2,72,8,128]{3,2,1,0:T(8,128)}, u32[]{:S(2)}) copy-start(f32[2,72,8,128]{3,2,1,0:T(8,128)} %param.12) | copy-start | bytes 1769476
  71.7 3.4 %copy-start.13 = (pred[72]{0:T(512)(128)(4,1)S(1)}, pred[72]{0:T(512)(128)(4,1)}, u32[]{:S(2)}) copy-start(pred[72]{0:T(512)(128)(4,1)} %copy-done.12) | copy-start | bytes 220
  79.7 6.3 %collective-permute-start.4 = (f32[2,72,8,1]{1,2,3,0:T(8,128)S(1)}, f32[2,72,8,1]{1,2,3,0:T(8,128)S(1)}, u32[]{:S(2)}, u32[]{:S(2)}) collective-permute-start(f32[2,72,8,1]{1,2,3,0:T(8,128)S(1)} %copy.49), channel_id=1, source_target_pairs={{0,32},{32,64},{64,96},{96,128},{128,160},{160,192},{192,224},{224... | collective-permute-start | bytes 13832 | tf_op jit(solution)/shard_map/ppermute | solution.py:16
  83.5 8.2 %collective-permute-start.5 = (f32[2,72,8,1]{1,2,3,0:T(8,128)S(1)}, f32[2,72,8,1]{1,2,3,0:T(8,128)S(1)}, u32[]{:S(2)}, u32[]{:S(2)}) collective-permute-start(f32[2,72,8,1]{1,2,3,0:T(8,128)S(1)} %copy.50), channel_id=1, source_target_pairs={{32,0},{64,32},{96,64},{128,96},{160,128},{192,160},{224,192},{256... | collective-permute-start | bytes 13832 | tf_op jit(solution)/shard_map/ppermute | solution.py:19
  92.8 6.2 %copy-start.6 = (f32[71,8,128]{2,1,0:T(8,128)S(1)}, f32[71,8,128]{2,1,0:T(8,128)}, u32[]{:S(2)}) copy-start(f32[71,8,128]{2,1,0:T(8,128)} %convert_multiply_fusion) | copy-start | bytes 872452
  94.3 16.1 %copy-start.2 = (f32[2,72,8,1]{3,0,2,1:T(2,128)S(1)}, f32[2,72,8,1]{3,0,2,1:T(2,128)}, u32[]{:S(2)}) copy-start(f32[2,72,8,1]{3,0,2,1:T(2,128)} %copy.52) | copy-start | bytes 13828
  94.3 6.3 %collective-permute-start.6 = (f32[2,72,1,130]{3,0,2,1:T(2,128)S(1)}, f32[2,72,1,130]{3,0,2,1:T(2,128)S(1)}, u32[]{:S(2)}, u32[]{:S(2)}) collective-permute-start(f32[2,72,1,130]{3,0,2,1:T(2,128)S(1)} %get-tuple-element.30), channel_id=1, source_target_pairs={{1,0},{2,1},{3,2},{4,3},{5,4},{6,5},{7,6},{8,7},{9,8},{10,9},{11,1... | collective-permute-start | bytes 224648 | tf_op jit(solution)/shard_map/ppermute | solution.py:19
  96.4 14.1 %collective-permute-start.7 = (f32[2,72,1,130]{3,0,2,1:T(2,128)S(1)}, f32[2,72,1,130]{3,0,2,1:T(2,128)S(1)}, u32[]{:S(2)}, u32[]{:S(2)}) collective-permute-start(f32[2,72,1,130]{3,0,2,1:T(2,128)S(1)} %get-tuple-element.29), channel_id=1, source_target_pairs={{0,1},{1,2},{2,3},{3,4},{4,5},{5,6},{6,7},{7,8},{8,9},{9,10},{10,1... | collective-permute-start | bytes 224648 | tf_op jit(solution)/shard_map/ppermute | solution.py:16
  (2 other events, 1.4 us)
where the time goes:
time: 121 us; the launch traced here: 120 us
  starting transfers between devices  46.3 us (38%)
  other arithmetic  28.1 us (23%)
  waiting for transfers between devices  24.6 us (20%)
  local copies, waits for them, and re-layouts  17.5 us (14%)
  matrix products  3.41 us (3%)
    all_to_all x1, starting transfers between devices, per_device(): lax.all_to_all(outgoing, 'comp', split_axis=0, concat_axis=0, tiled=True)  18.8 us
    ppermute x4, waiting for transfers between devices, with_halo(): lax.ppermute(lax.slice_in_dim(block, block.shape[dim] - width, None, axis...  18.1 us
    ppermute x4, starting transfers between devices, with_halo(): lax.ppermute(lax.slice_in_dim(block, block.shape[dim] - width, None, axis...  16 us
    ppermute x4, starting transfers between devices, with_halo(): lax.ppermute(lax.slice_in_dim(block, 0, width, axis=dim), axis, backward)  11.5 us
    concatenate x4, other arithmetic, with_halo(): block = jnp.concatenate([low, block, high], axis=dim)  9.52 us
    add x2, other arithmetic, advance(): updated = centre + lateral * laplace + mixing  8.84 us
    ppermute x4, waiting for transfers between devices, with_halo(): lax.ppermute(lax.slice_in_dim(block, 0, width, axis=dim), axis, backward)  6.51 us
    slice x3, local copies, waits for them, and re-layouts, with_halo(): lax.slice_in_dim(block, block.shape[dim] - width, None, axis=dim)  5.25 us
  transfers between devices with their start and end apart: 9, of which 4 were waited for; matrix products, arithmetic and copies ran while one was open for 20% of the time, Pallas kernels for 0%

commit v1 on v0

v1 whole, which is shorter than its diff:
```python
import functools

import jax
import jax.numpy as jnp
from jax import lax
from jax.experimental import pallas as pl
from jax.experimental.pallas import tpu as pltpu
from jax.sharding import PartitionSpec as P

OLEV = 60
CHUNK = 24
MESH = pl.DeviceIdType.MESH


def tile_of(index):
    return pl.ds(pl.multiple_of(index * 8, 8), 8)


def kernel(
    levels,
    tracers,
    fields,
    lateral,
    vertical,
    gain,
    send_slots,
    recv_slots,
    weights,
    out,
    first,
    second,
    lat,
    ver,
    rate,
    surf,
    blocks,
    outgoing,
    incoming,
    spread,
    wts,
    forcing,
    gains,
    sends,
    recvs,
    x_out,
    x_in,
    y_out,
    y_in,
    x0_out,
    x0_in,
    y0_out,
    y0_in,
    load_sem,
    remap_send,
    remap_recv,
    x_send,
    x_recv,
    y_send,
    y_recv,
    x0_send,
    x0_recv,
    y0_send,
    y0_recv,
):
    rows = lax.axis_size("comp")
    tiles = lax.axis_size("tile")
    atmos = 3 * rows // 4
    ocean = rows - atmos
    row = lax.axis_index("comp")
    tile = lax.axis_index("tile")
    left = lax.rem(tile + tiles - 1, tiles)
    right = lax.rem(tile + 1, tiles)
    is_ocean = row >= atmos
    is_atmos = row < atmos
    has_lower = jnp.logical_and(row != 0, row != atmos)
    has_upper = jnp.logical_and(row != atmos - 1, row != rows - 1)
    no_lower = jnp.logical_or(row == 0, row == atmos)
    no_upper = jnp.logical_or(row == atmos - 1, row == rows - 1)
    live_levels = jnp.where(is_ocean, OLEV, levels)
    chunks = levels // CHUNK
    lane = lax.broadcasted_iota(jnp.int32, (8, 128), 1)
    sub = lax.broadcasted_iota(jnp.int32, (8, 128), 0)

    loads = [
        pltpu.make_async_copy(source, target, load_sem.at[place])
        for place, (source, target) in enumerate(
            [
                (fields, surf),
                (send_slots, sends),
                (tracers, first),
                (vertical, ver),
                (lateral, lat),
                (recv_slots, recvs),
                (gain, gains),
            ]
        )
    ]
    get_fields, get_sends, get_tracers, get_vertical, get_lateral, get_recvs, get_gain = loads
    for load in loads:
        load.start()

    def get_weights(base, count):
        return pltpu.make_async_copy(
            weights.at[pl.ds(base, count)], wts.at[pl.ds(0, count)], load_sem.at[7]
        )

    @pl.when(is_ocean)
    def _():
        get_weights(0, atmos).start()

    @pl.when(is_atmos)
    def _():
        get_weights(atmos, ocean).start()

    barrier = pltpu.get_barrier_semaphore()

    def greet(to_row, to_tile):
        pl.semaphore_signal(barrier, inc=1, device_id=(to_row, to_tile), device_id_type=MESH)

    greet(row, left)
    greet(row, right)

    @pl.when(has_lower)
    def _():
        greet(row - 1, tile)

    @pl.when(has_upper)
    def _():
        greet(row + 1, tile)

    @pl.when(is_ocean)
    def _():
        for partner in range(atmos):
            greet(partner, tile)

    @pl.when(is_atmos)
    def _():
        for partner in range(atmos, rows):
            greet(partner, tile)

    get_fields.wait()
    get_sends.wait()
    for block in range(8):
        picked = surf[pl.ds(block, 4, stride=8), :]
        blocks[block, 0:4, :] = picked
        blocks[block, 4:8, :] = picked
    blocks[8] = jnp.zeros((8, 128), jnp.float32)

    def fill(base, count):
        def one(place, carry):
            slot0 = sends[0, base + place]
            slot1 = sends[1, base + place]
            slot0 = jnp.where(slot0 < 0, 8, slot0)
            slot1 = jnp.where(slot1 < 0, 8, slot1)
            outgoing[place] = jnp.where(sub < 4, blocks[slot0], blocks[slot1])
            return carry

        lax.fori_loop(0, count, one, 0, unroll=4)

    @pl.when(is_ocean)
    def _():
        fill(0, atmos)

    @pl.when(is_atmos)
    def _():
        fill(atmos, ocean)

    def pack_x(step, chunk, source):
        for var in range(2):
            start = (var * levels + chunk * CHUNK) * 8
            here = pl.ds(pl.multiple_of(chunk * CHUNK, 8), CHUNK)
            x_out[step, 1, var, here, :] = source[pl.ds(start, CHUNK, stride=8), :]
            x_out[step, 0, var, here, :] = source[pl.ds(start + 7, CHUNK, stride=8), :]

    def add_lanes(low, high, value, entry):
        turned = pltpu.roll(value, 2 * entry, 1) if entry else value
        low = jnp.where(lane == 2 * entry, turned, low)
        high = jnp.where(lane == (2 * entry + 127) % 128, turned, high)
        return low, high

    def put_y(target, wall, low, high):
        target[1] = low
        target[0] = high

        @pl.when(no_lower)
        def _():
            wall[0] = pltpu.roll(low, 127, 1)

        @pl.when(no_upper)
        def _():
            wall[1] = pltpu.roll(high, 1, 1)

    def copy_x(step, chunk, side):
        here = pl.ds(pl.multiple_of(chunk * CHUNK, 8), CHUNK)
        return pltpu.make_async_remote_copy(
            src_ref=x_out.at[step, side, :, here, :],
            dst_ref=x_in.at[step, side, :, here, :],
            send_sem=x_send.at[step, side, chunk],
            recv_sem=x_recv.at[step, side, chunk],
            device_id=(row, left if side else right),
            device_id_type=MESH,
        )

    def copy_y(step, chunk, side):
        return pltpu.make_async_remote_copy(
            src_ref=y_out.at[step, chunk, side],
            dst_ref=y_in.at[step, chunk, side],
            send_sem=y_send.at[step, side, chunk],
            recv_sem=y_recv.at[step, side, chunk],
            device_id=(row - 1 if side else row + 1, tile),
            device_id_type=MESH,
        )

    def copy_x0(side):
        return pltpu.make_async_remote_copy(
            src_ref=x0_out.at[side],
            dst_ref=x0_in.at[side],
            send_sem=x0_send.at[side],
            recv_sem=x0_recv.at[side],
            device_id=(row, left if side else right),
            device_id_type=MESH,
        )

    def copy_y0(side):
        return pltpu.make_async_remote_copy(
            src_ref=y0_out.at[side],
            dst_ref=y0_in.at[side],
            send_sem=y0_send.at[side],
            recv_sem=y0_recv.at[side],
            device_id=(row - 1 if side else row + 1, tile),
            device_id_type=MESH,
        )

    def start_edges(step, chunk):
        copy_x(step, chunk, 0).start()
        copy_x(step, chunk, 1).start()

        @pl.when(has_lower)
        def _():
            copy_y(step, chunk, 1).start()

        @pl.when(has_upper)
        def _():
            copy_y(step, chunk, 0).start()

    def await_edges(step, chunk):
        copy_x(step, chunk, 0).wait_recv()
        copy_x(step, chunk, 1).wait_recv()

        @pl.when(has_lower)
        def _():
            copy_y(step, chunk, 0).wait_recv()

        @pl.when(has_upper)
        def _():
            copy_y(step, chunk, 1).wait_recv()

    def end_edges(step, chunk):
        copy_x(step, chunk, 0).wait_send()
        copy_x(step, chunk, 1).wait_send()

        @pl.when(has_lower)
        def _():
            copy_y(step, chunk, 1).wait_send()

        @pl.when(has_upper)
        def _():
            copy_y(step, chunk, 0).wait_send()

    get_tracers.wait()

    def pack_first(turn, carry):
        chunk = chunks - 1 - turn
        pack_x(0, chunk, first)
        low = high = jnp.zeros((8, 128), jnp.float32)
        for level in range(CHUNK):
            for var in range(2):
                value = first[tile_of(var * levels + chunk * CHUNK + level), :]
                low, high = add_lanes(low, high, value, 2 * level + var)
        put_y(y_out.at[0, chunk], y_in.at[0, chunk], low, high)
        return carry

    lax.fori_loop(0, chunks, pack_first, 0)

    others = jnp.where(is_ocean, atmos, ocean)
    beside = has_lower.astype(jnp.int32) + has_upper.astype(jnp.int32)
    pl.semaphore_wait(barrier, others + beside + 2)

    def copy_block(base, count, own_base, place):
        return pltpu.make_async_remote_copy(
            src_ref=outgoing.at[place],
            dst_ref=incoming.at[row - own_base],
            send_sem=remap_send,
            recv_sem=remap_recv,
            device_id=(base + place, tile),
            device_id_type=MESH,
        )

    def send_blocks(base, count, own_base):
        def one(turn, carry):
            place = lax.rem(turn + row + tile, count)
            copy_block(base, count, own_base, place).start()
            return carry

        lax.fori_loop(0, count, one, 0)

    @pl.when(is_ocean)
    def _():
        send_blocks(0, atmos, atmos)

    @pl.when(is_atmos)
    def _():
        send_blocks(atmos, ocean, 0)

    def send_first(turn, carry):
        start_edges(0, chunks - 1 - turn)
        return carry

    lax.fori_loop(0, chunks, send_first, 0)

    get_vertical.wait()
    get_lateral.wait()
    rate[0] = jnp.zeros((8, 128), jnp.float32)
    rate[levels] = jnp.zeros((8, 128), jnp.float32)

    def one_rate(level, carry):
        value = ver[level].astype(jnp.float32)
        rate[level + 1] = jnp.where(level + 1 < live_levels, value, 0.0)
        return carry

    lax.fori_loop(0, levels - 1, one_rate, 0, unroll=8)

    def advance(step, chunk, source, target, merged, edges):
        lateral_here = lat[...].astype(jnp.float32)
        base = chunk * CHUNK
        previous = [None, None]
        centre = [None, None]
        low = high = jnp.zeros((8, 128), jnp.float32)
        for var in range(2):
            centre[var] = source[tile_of(var * levels + base), :]
            above = source[tile_of(var * levels + jnp.maximum(base - 1, 0)), :]
            previous[var] = rate[base] * (centre[var] - above)
        for level in range(CHUNK):
            here = base + level
            mixing = rate[here + 1]
            spreading = jnp.where(here < live_levels, lateral_here, 0.0)
            for var in range(2):
                entry = 2 * level + var
                after = jnp.minimum(here + 1, levels - 1) if level == CHUNK - 1 else here + 1
                value = centre[var]
                below = source[tile_of(var * levels + after), :]
                x_low = jnp.broadcast_to(x_in[step, 0, var, pl.ds(here, 1), :], (8, 128))
                x_high = jnp.broadcast_to(x_in[step, 1, var, pl.ds(here, 1), :], (8, 128))
                ends = pltpu.roll(merged, 127 - 2 * entry, 1)
                sides = (
                    jnp.where(sub == 0, x_low, pltpu.roll(value, 1, 0))
                    + jnp.where(sub == 7, x_high, pltpu.roll(value, 7, 0))
                ) + (
                    jnp.where(lane == 0, ends, pltpu.roll(value, 1, 1))
                    + jnp.where(lane == 127, ends, pltpu.roll(value, 127, 1))
                )
                down = mixing * (below - value)
                result = value + spreading * (sides - 4.0 * value) + (down - previous[var])
                target[tile_of(var * levels + here), :] = result
                if edges:
                    low, high = add_lanes(low, high, result, entry)
                centre[var] = below
                previous[var] = down
        return low, high

    def merge(low, high):
        return jnp.where(lane % 2 == 1, pltpu.roll(low, 2, 1), high)

    def step_one(turn, carry):
        chunk = chunks - 1 - turn
        await_edges(0, chunk)
        merged = merge(y_in[0, chunk, 0], y_in[0, chunk, 1])
        low, high = advance(0, chunk, first, second, merged, True)
        pack_x(1, chunk, second)
        put_y(y_out.at[1, chunk], y_in.at[1, chunk], low, high)
        start_edges(1, chunk)
        return carry

    lax.fori_loop(0, chunks, step_one, 0)

    get_recvs.wait()
    get_gain.wait()

    def remap(base, count):
        pltpu.make_async_copy(
            incoming.at[pl.ds(0, count)], incoming.at[pl.ds(0, count)], remap_recv
        ).wait()

        def one(place, carry):
            for slot in range(2):
                lands = sub == recvs[slot, base + place]
                column = pl.ds(pl.multiple_of((place * 2 + slot) * 128, 128), 128)
                for pair in range(2):
                    value = jnp.concatenate(
                        [
                            jnp.where(
                                lands,
                                jnp.broadcast_to(
                                    incoming[place, slot * 4 + field : slot * 4 + field + 1, :],
                                    (8, 128),
                                ),
                                0.0,
                            )
                            for field in (2 * pair, 2 * pair + 1)
                        ],
                        axis=0,
                    )
                    coarse = value.astype(jnp.bfloat16)
                    fine = (value - coarse.astype(jnp.float32)).astype(jnp.bfloat16)
                    spread[16 * pair : 16 * pair + 16, column] = coarse
                    spread[32 + 16 * pair : 48 + 16 * pair, column] = fine
            return carry

        lax.fori_loop(0, count, one, 0, unroll=2)
        get_weights(base, count).wait()
        total = jnp.dot(
            spread[:, : count * 256],
            wts[:count].reshape(count * 256, 128),
            preferred_element_type=jnp.float32,
        )
        remapped = total[:32] + total[32:]
        low = high = jnp.zeros((8, 128), jnp.float32)
        values = []
        for var in range(2):
            force = gains[var, 0] * remapped[:8]
            for field in range(1, 4):
                force = force + gains[var, field] * remapped[8 * field : 8 * field + 8]
            forcing[var] = force
            value = second[tile_of(var * levels), :] + force
            second[tile_of(var * levels), :] = value
            low, high = add_lanes(low, high, value, var)
            values.append(value)
        x0_out[1] = jnp.where(sub == 0, values[0][0:1, :], values[1][0:1, :])
        x0_out[0] = jnp.where(sub == 0, values[0][7:8, :], values[1][7:8, :])
        put_y(y0_out, y0_in, low, high)

    @pl.when(is_ocean)
    def _():
        remap(0, atmos)

    @pl.when(is_atmos)
    def _():
        remap(atmos, ocean)

    copy_x0(0).start()
    copy_x0(1).start()

    @pl.when(has_lower)
    def _():
        copy_y0(1).start()

    @pl.when(has_upper)
    def _():
        copy_y0(0).start()

    def step_two(turn, carry):
        chunk = chunks - 1 - turn
        await_edges(1, chunk)
        merged = merge(y_in[1, chunk, 0], y_in[1, chunk, 1])
        advance(1, chunk, second, out, merged, False)
        return carry

    lax.fori_loop(0, chunks - 1, step_two, 0)

    await_edges(1, 0)
    copy_x0(0).wait_recv()
    copy_x0(1).wait_recv()

    @pl.when(has_lower)
    def _():
        copy_y0(0).wait_recv()

    @pl.when(has_upper)
    def _():
        copy_y0(1).wait_recv()

    for side in range(2):
        for var in range(2):
            x_in[1, side, var, 0:1, :] = x0_in[side, var : var + 1, :]
    merged = jnp.where(
        lane < 4, merge(y0_in[0], y0_in[1]), merge(y_in[1, 0, 0], y_in[1, 0, 1])
    )
    advance(1, 0, second, out, merged, False)
    for var in range(2):
        out[tile_of(var * levels), :] += forcing[var]

    for step in range(2):

        def end(chunk, carry):
            end_edges(step, chunk)
            return carry

        lax.fori_loop(0, chunks, end, 0)
    copy_x0(0).wait_send()
    copy_x0(1).wait_send()

    @pl.when(has_lower)
    def _():
        copy_y0(1).wait_send()

    @pl.when(has_upper)
    def _():
        copy_y0(0).wait_send()

    @pl.when(is_ocean)
    def _():
        pltpu.make_async_copy(
            outgoing.at[pl.ds(0, atmos)], outgoing.at[pl.ds(0, atmos)], remap_send
        ).wait()

    @pl.when(is_atmos)
    def _():
        pltpu.make_async_copy(
            outgoing.at[pl.ds(0, ocean)], outgoing.at[pl.ds(0, ocean)], remap_send
        ).wait()


def per_device(
    tracers,
    surface_fields,
    lateral_rate,
    vertical_rate,
    coupling_gain,
    send_slots,
    recv_slots,
    remap_weights,
):
    rows = lax.axis_size("comp")
    atmos = 3 * rows // 4
    levels = tracers.shape[1]
    chunks = levels // CHUNK
    cells = 2 * levels * 8
    f32, bf16, i32 = jnp.float32, jnp.bfloat16, jnp.int32
    hbm = pl.BlockSpec(memory_space=pltpu.HBM)
    dma = pltpu.SemaphoreType.DMA
    result = pl.pallas_call(
        functools.partial(kernel, levels),
        out_shape=jax.ShapeDtypeStruct((cells, 128), f32),
        in_specs=[hbm] * 8,
        out_specs=pl.BlockSpec(memory_space=pltpu.VMEM),
        scratch_shapes=[
            pltpu.VMEM((cells, 128), f32),
            pltpu.VMEM((cells, 128), f32),
            pltpu.VMEM((8, 128), bf16),
            pltpu.VMEM((levels - 1, 8, 128), bf16),
            pltpu.VMEM((levels + 1, 8, 128), f32),
            pltpu.VMEM((32, 128), f32),
            pltpu.VMEM((9, 8, 128), f32),
            pltpu.VMEM((atmos, 8, 128), f32),
            pltpu.VMEM((atmos, 8, 128), f32),
            pltpu.VMEM((64, atmos * 256), bf16),
            pltpu.VMEM((atmos, 256, 128), bf16),
            pltpu.VMEM((2, 8, 128), f32),
            pltpu.SMEM((2, 4), f32),
            pltpu.SMEM((2, rows), i32),
            pltpu.SMEM((2, rows), i32),
            pltpu.VMEM((2, 2, 2, levels, 128), f32),
            pltpu.VMEM((2, 2, 2, levels, 128), f32),
            pltpu.VMEM((2, chunks, 2, 8, 128), f32),
            pltpu.VMEM((2, chunks, 2, 8, 128), f32),
            pltpu.VMEM((2, 8, 128), f32),
            pltpu.VMEM((2, 8, 128), f32),
            pltpu.VMEM((2, 8, 128), f32),
            pltpu.VMEM((2, 8, 128), f32),
            dma((8,)),
            dma,
            dma,
            dma((2, 2, chunks)),
            dma((2, 2, chunks)),
            dma((2, 2, chunks)),
            dma((2, 2, chunks)),
            dma((2,)),
            dma((2,)),
            dma((2,)),
            dma((2,)),
        ],
        compiler_params=pltpu.CompilerParams(
            collective_id=0, has_side_effects=True, vmem_limit_bytes=60 * 1024 * 1024
        ),
        cost_estimate=pl.CostEstimate(
            flops=60_000_000, bytes_accessed=4_000_000, transcendentals=0
        ),
    )(
        tracers.reshape(cells, 128),
        surface_fields.reshape(32, 128),
        lateral_rate,
        vertical_rate,
        coupling_gain[0],
        jnp.transpose(send_slots[0, :, 0]),
        jnp.transpose(recv_slots[0, :, 0]),
        remap_weights.reshape(rows, 256, 128),
    )
    return result.reshape(tracers.shape)


def solution(mesh):
    return jax.shard_map(
        per_device,
        mesh=mesh,
        in_specs=(
            P(None, None, "tile", "comp"),
            P(None, "tile", "comp"),
            P("tile", "comp"),
            P(None, "tile", "comp"),
            P("comp", None, None),
            P("comp", None, "tile", None),
            P("comp", None, "tile", None),
            P("comp", None, "tile", None, None, None),
        ),
        out_specs=P(None, None, "tile", "comp"),
        check_vma=False,
    )
```

time: 121 us -> 36.3 us (0.30)
  the two profiles are of different devices: /device:TPU:14 before, /device:TPU:6 now
where the time goes in v1:
time: 36.3 us; the launch traced here: 36.1 us
  Pallas kernels  34.2 us (94%)
  local copies, waits for them, and re-layouts  1.92 us (5%)
    pallas_call x1, Pallas kernels, per_device(): pl.pallas_call(functools.partial(kernel, levels), out_shape=jax.ShapeDtyp...  34.2 us
    unnamed x1, local copies, waits for them, and re-layouts  1.92 us

profile of v1, /device:TPU:6, one launch (start us, length us, event | category | flops | bytes accessed | tf_op | source)
XLA Modules:
  0.0 36.1 jit_solution(119313161239274480)
XLA Ops:
  0.0 34.2 %shard_map.82 = f32[1152,128]{1,0:T(8,128)} custom-call(f32[1152,128]{1,0:T(8,128)} %bitcast.13, f32[32,128]{1,0:T(8,128)} %bitcast.14, bf16[8,128]{1,0:T(8,128)(2,1)} %lateral.1, bf16[71,8,128]{2,1,0:T(8,128)(2,1)} %vertical.1, f32[2,4]{1,0:T(2,128)} %bitcast.15, s32[2,32]{1,0:T(2,128)} %bitcast.16, s32[2,32]{1,0:T(2,128)} %bitcast.17, ...), custom_call_target="tpu_custom_call" | custom-call | flops 60000000 | bytes 4000000 | tf_op jit(solution)/shard_map/pallas_call | solution.py:541
  34.2 1.9 %copy.10 = f32[2,72,8,128]{3,2,1,0:T(8,128)} copy(f32[2,72,8,128]{3,2,1,0:T(8,128)} %bitcast.11) | data formatting | bytes 1179648

commit v2 on v1

--- a/solution.py
+++ b/solution.py
@@ -9,6 +9,7 @@
 
 OLEV = 60
 CHUNK = 24
+RELAY = 2
 MESH = pl.DeviceIdType.MESH
 
 
@@ -61,6 +62,9 @@
     x0_recv,
     y0_send,
     y0_recv,
+    here,
+    near,
+    go,
 ):
     rows = lax.axis_size("comp")
     tiles = lax.axis_size("tile")
@@ -117,53 +121,64 @@
     def greet(to_row, to_tile):
         pl.semaphore_signal(barrier, inc=1, device_id=(to_row, to_tile), device_id_type=MESH)
 
-    greet(row, left)
-    greet(row, right)
-
-    @pl.when(has_lower)
-    def _():
-        greet(row - 1, tile)
-
-    @pl.when(has_upper)
-    def _():
-        greet(row + 1, tile)
-
-    @pl.when(is_ocean)
-    def _():
-        for partner in range(atmos):
-            greet(partner, tile)
-
     @pl.when(is_atmos)
     def _():
         for partner in range(atmos, rows):
             greet(partner, tile)
-
-    get_fields.wait()
-    get_sends.wait()
-    for block in range(8):
-        picked = surf[pl.ds(block, 4, stride=8), :]
-        blocks[block, 0:4, :] = picked
-        blocks[block, 4:8, :] = picked
-    blocks[8] = jnp.zeros((8, 128), jnp.float32)
-
-    def fill(base, count):
-        def one(place, carry):
-            slot0 = sends[0, base + place]
-            slot1 = sends[1, base + place]
-            slot0 = jnp.where(slot0 < 0, 8, slot0)
-            slot1 = jnp.where(slot1 < 0, 8, slot1)
-            outgoing[place] = jnp.where(sub < 4, blocks[slot0], blocks[slot1])
-            return carry
-
-        lax.fori_loop(0, count, one, 0, unroll=4)
+        greet(row, left)
+        greet(row, right)
+
+        @pl.when(has_lower)
+        def _():
+            greet(row - 1, tile)
+
+        @pl.when(has_upper)
+        def _():
+            greet(row + 1, tile)
+
+    def list_blocks():
+        get_fields.wait()
+        get_sends.wait()
+        for block in range(8):
+            picked = surf[pl.ds(block, 4, stride=8), :]
+            blocks[block, 0:4, :] = picked
+            blocks[block, 4:8, :] = picked
+        blocks[8] = jnp.zeros((8, 128), jnp.float32)
+
+    def fill(base, place):
+        slot0 = sends[0, base + place]
+        slot1 = sends[1, base + place]
+        slot0 = jnp.where(slot0 < 0, 8, slot0)
+        slot1 = jnp.where(slot1 < 0, 8, slot1)
+        outgoing[place] = jnp.where(sub < 4, blocks[slot0], blocks[slot1])
+
+    def send_block(base, place, own_base):
+        pltpu.make_async_remote_copy(
+            src_ref=outgoing.at[place],
+            dst_ref=incoming.at[row - own_base],
+            send_sem=remap_send,
+            recv_sem=remap_recv,
+            device_id=(base + place, tile),
+            device_id_type=MESH,
+        ).start()
 
     @pl.when(is_ocean)
     def _():
-        fill(0, atmos)
+        list_blocks()
+        pl.semaphore_wait(barrier, atmos)
+        pl.semaphore_signal(here, inc=1, device_id=(RELAY, tile), device_id_type=MESH)
+        for place in range(atmos):
+            fill(0, place)
+            send_block(0, place, atmos)
 
     @pl.when(is_atmos)
     def _():
-        fill(atmos, ocean)
+        list_blocks()
+        for place in range(ocean):
+            fill(atmos, place)
+        pl.semaphore_wait(
+            barrier, 2 + has_lower.astype(jnp.int32) + has_upper.astype(jnp.int32)
+        )
 
     def pack_x(step, chunk, source):
         for var in range(2):
@@ -282,35 +297,14 @@
 
     lax.fori_loop(0, chunks, pack_first, 0)
 
-    others = jnp.where(is_ocean, atmos, ocean)
-    beside = has_lower.astype(jnp.int32) + has_upper.astype(jnp.int32)
-    pl.semaphore_wait(barrier, others + beside + 2)
-
-    def copy_block(base, count, own_base, place):
-        return pltpu.make_async_remote_copy(
-            src_ref=outgoing.at[place],
-            dst_ref=incoming.at[row - own_base],
-            send_sem=remap_send,
-            recv_sem=remap_recv,
-            device_id=(base + place, tile),
-            device_id_type=MESH,
-        )
-
-    def send_blocks(base, count, own_base):
-        def one(turn, carry):
-            place = lax.rem(turn + row + tile, count)
-            copy_block(base, count, own_base, place).start()
-            return carry
-
-        lax.fori_loop(0, count, one, 0)
+    def await_blocks(count):
+        pltpu.make_async_copy(
+            incoming.at[pl.ds(0, count)], incoming.at[pl.ds(0, count)], remap_recv
+        ).wait()
 
     @pl.when(is_ocean)
     def _():
-        send_blocks(0, atmos, atmos)
-
-    @pl.when(is_atmos)
-    def _():
-        send_blocks(atmos, ocean, 0)
+        pl.semaphore_wait(go, 1)
 
     def send_first(turn, carry):
         start_edges(0, chunks - 1 - turn)
@@ -329,6 +323,16 @@
         return carry
 
     lax.fori_loop(0, levels - 1, one_rate, 0, unroll=8)
+
+    def sides_of(value, x_low, x_high, merged, entry):
+        ends = pltpu.roll(merged, 127 - 2 * entry, 1)
+        return (
+            jnp.where(sub == 0, x_low, pltpu.roll(value, 1, 0))
+            + jnp.where(sub == 7, x_high, pltpu.roll(value, 7, 0))
+        ) + (
+            jnp.where(lane == 0, ends, pltpu.roll(value, 1, 1))
+            + jnp.where(lane == 127, ends, pltpu.roll(value, 127, 1))
+        )
 
     def advance(step, chunk, source, target, merged, edges):
         lateral_here = lat[...].astype(jnp.float32)
@@ -351,14 +355,7 @@
                 below = source[tile_of(var * levels + after), :]
                 x_low = jnp.broadcast_to(x_in[step, 0, var, pl.ds(here, 1), :], (8, 128))
                 x_high = jnp.broadcast_to(x_in[step, 1, var, pl.ds(here, 1), :], (8, 128))
-                ends = pltpu.roll(merged, 127 - 2 * entry, 1)
-                sides = (
-                    jnp.where(sub == 0, x_low, pltpu.roll(value, 1, 0))
-                    + jnp.where(sub == 7, x_high, pltpu.roll(value, 7, 0))
-                ) + (
-                    jnp.where(lane == 0, ends, pltpu.roll(value, 1, 1))
-                    + jnp.where(lane == 127, ends, pltpu.roll(value, 127, 1))
-                )
+                sides = sides_of(value, x_low, x_high, merged, entry)
                 down = mixing * (below - value)
                 result = value + spreading * (sides - 4.0 * value) + (down - previous[var])
                 target[tile_of(var * levels + here), :] = result
@@ -381,16 +378,11 @@
         start_edges(1, chunk)
         return carry
 
-    lax.fori_loop(0, chunks, step_one, 0)
 
     get_recvs.wait()
     get_gain.wait()
 
     def remap(base, count):
-        pltpu.make_async_copy(
-            incoming.at[pl.ds(0, count)], incoming.at[pl.ds(0, count)], remap_recv
-        ).wait()
-
         def one(place, carry):
             for slot in range(2):
                 lands = sub == recvs[slot, base + place]
@@ -431,32 +423,63 @@
             for field in range(1, 4):
                 force = force + gains[var, field] * remapped[8 * field : 8 * field + 8]
             forcing[var] = force
-            value = second[tile_of(var * levels), :] + force
-            second[tile_of(var * levels), :] = value
-            low, high = add_lanes(low, high, value, var)
-            values.append(value)
+            low, high = add_lanes(low, high, force, var)
+            values.append(force)
         x0_out[1] = jnp.where(sub == 0, values[0][0:1, :], values[1][0:1, :])
         x0_out[0] = jnp.where(sub == 0, values[0][7:8, :], values[1][7:8, :])
         put_y(y0_out, y0_in, low, high)
 
-    @pl.when(is_ocean)
-    def _():
-        remap(0, atmos)
-
-    @pl.when(is_atmos)
-    def _():
-        remap(atmos, ocean)
-
-    copy_x0(0).start()
-    copy_x0(1).start()
-
-    @pl.when(has_lower)
-    def _():
-        copy_y0(1).start()
-
-    @pl.when(has_upper)
-    def _():
-        copy_y0(0).start()
+    def force():
+        @pl.when(row == RELAY)
+        def _():
+            pl.semaphore_wait(here, ocean)
+            for side in (left, right):
+                pl.semaphore_signal(near, inc=1, device_id=(row, side), device_id_type=MESH)
+            pl.semaphore_wait(near, 2)
+            for partner in range(atmos, rows):
+                pl.semaphore_signal(go, inc=1, device_id=(partner, tile), device_id_type=MESH)
+
+        @pl.when(is_atmos)
+        def _():
+            await_blocks(ocean)
+            remap(atmos, ocean)
+
+        @pl.when(is_ocean)
+        def _():
+            await_blocks(atmos)
+            remap(0, atmos)
+
+        copy_x0(0).start()
+        copy_x0(1).start()
+
+        @pl.when(has_lower)
+        def _():
+            copy_y0(1).start()
+
+        @pl.when(has_upper)
+        def _():
+            copy_y0(0).start()
+
+        @pl.when(is_atmos)
+        def _():
+            for place in range(ocean):
+                send_block(atmos, place, 0)
+
+    forced_first = jnp.logical_and(row >= 2 * atmos // 3, is_atmos)
+    steps_first = jnp.where(forced_first, 1, 0)
+
+    def phase(turn, carry):
+        @pl.when(turn == steps_first)
+        def _():
+            lax.fori_loop(0, chunks, step_one, 0)
+
+        @pl.when(turn != steps_first)
+        def _():
+            force()
+
+        return carry
+
+    lax.fori_loop(0, 2, phase, 0)
 
     def step_two(turn, carry):
         chunk = chunks - 1 - turn
@@ -465,30 +488,7 @@
         advance(1, chunk, second, out, merged, False)
         return carry
 
-    lax.fori_loop(0, chunks - 1, step_two, 0)
-
-    await_edges(1, 0)
-    copy_x0(0).wait_recv()
-    copy_x0(1).wait_recv()
-
-    @pl.when(has_lower)
-    def _():
-        copy_y0(0).wait_recv()
-
-    @pl.when(has_upper)
-    def _():
-        copy_y0(1).wait_recv()
-
-    for side in range(2):
-        for var in range(2):
-            x_in[1, side, var, 0:1, :] = x0_in[side, var : var + 1, :]
-    merged = jnp.where(
-        lane < 4, merge(y0_in[0], y0_in[1]), merge(y_in[1, 0, 0], y_in[1, 0, 1])
-    )
-    advance(1, 0, second, out, merged, False)
-    for var in range(2):
-        out[tile_of(var * levels), :] += forcing[var]
-
+    lax.fori_loop(0, chunks, step_two, 0)
     for step in range(2):
 
         def end(chunk, carry):
@@ -496,6 +496,30 @@
             return carry
 
         lax.fori_loop(0, chunks, end, 0)
+
+    copy_x0(0).wait_recv()
+    copy_x0(1).wait_recv()
+
+    @pl.when(has_lower)
+    def _():
+        copy_y0(0).wait_recv()
+
+    @pl.when(has_upper)
+    def _():
+        copy_y0(1).wait_recv()
+
+    merged = merge(y0_in[0], y0_in[1])
+    for var in range(2):
+        force = forcing[var]
+        x_low = jnp.broadcast_to(x0_in[0, var : var + 1, :], (8, 128))
+        x_high = jnp.broadcast_to(x0_in[1, var : var + 1, :], (8, 128))
+        mixing = rate[1] * force
+        effect = lat[...].astype(jnp.float32) * (
+            sides_of(force, x_low, x_high, merged, var) - 4.0 * force
+        )
+        out[tile_of(var * levels), :] += 2.0 * force + (effect - mixing)
+        out[tile_of(var * levels + 1), :] += mixing
+
     copy_x0(0).wait_send()
     copy_x0(1).wait_send()
 
@@ -540,7 +564,7 @@
     dma = pltpu.SemaphoreType.DMA
     result = pl.pallas_call(
         functools.partial(kernel, levels),
-        out_shape=jax.ShapeDtypeStruct((cells, 128), f32),
+        out_shape=pltpu.VMEM((cells, 128), f32),
         in_specs=[hbm] * 8,
         out_specs=pl.BlockSpec(memory_space=pltpu.VMEM),
         scratch_shapes=[
@@ -578,22 +602,30 @@
             dma((2,)),
             dma((2,)),
             dma((2,)),
+            pltpu.SemaphoreType.REGULAR,
+            pltpu.SemaphoreType.REGULAR,
+            pltpu.SemaphoreType.REGULAR,
         ],
         compiler_params=pltpu.CompilerParams(
-            collective_id=0, has_side_effects=True, vmem_limit_bytes=60 * 1024 * 1024
+            collective_id=0, has_side_effects=True, vmem_limit_bytes=48 * 1024 * 1024
         ),
         cost_estimate=pl.CostEstimate(
             flops=60_000_000, bytes_accessed=4_000_000, transcendentals=0
         ),
     )(
-        tracers.reshape(cells, 128),
-        surface_fields.reshape(32, 128),
-        lateral_rate,
-        vertical_rate,
-        coupling_gain[0],
-        jnp.transpose(send_slots[0, :, 0]),
-        jnp.transpose(recv_slots[0, :, 0]),
-        remap_weights.reshape(rows, 256, 128),
+        *[
+            pltpu.with_memory_space_constraint(array, pltpu.HBM)
+            for array in (
+                tracers.reshape(cells, 128),
+                surface_fields.reshape(32, 128),
+                lateral_rate,
+                vertical_rate,
+                coupling_gain[0],
+                jnp.transpose(send_slots[0, :, 0]),
+                jnp.transpose(recv_slots[0, :, 0]),
+                remap_weights.reshape(rows, 256, 128),
+            )
+        ]
     )
     return result.reshape(tracers.shape)
 

time: 36.3 us -> 31.5 us (0.87)
  the two profiles are of different devices: /device:TPU:6 before, /device:TPU:768 now
where the time goes in v2:
time: 31.5 us; the launch traced here: 31.2 us
  Pallas kernels  30.4 us (97%)
  local copies, waits for them, and re-layouts  0.82 us (3%)
    pallas_call x1, Pallas kernels, per_device(): pl.pallas_call(functools.partial(kernel, levels), out_shape=pltpu.VMEM((c...  30.4 us
    unnamed x1, local copies, waits for them, and re-layouts  0.82 us

profile of v2, /device:TPU:768, one launch (start us, length us, event | category | flops | bytes accessed | tf_op | source)
XLA Modules:
  0.0 31.2 jit_solution(5367025674643048165)
XLA Ops:
  0.0 30.4 %shard_map.82 = f32[1152,128]{1,0:T(8,128)S(1)} custom-call(f32[1152,128]{1,0:T(8,128)} %bitcast.13, f32[32,128]{1,0:T(8,128)} %bitcast.14, bf16[8,128]{1,0:T(8,128)(2,1)} %lateral.1, bf16[71,8,128]{2,1,0:T(8,128)(2,1)} %vertical.1, f32[2,4]{1,0:T(2,128)} %bitcast.15, s32[2,32]{1,0:T(2,128)} %bitcast.16, s32[2,32]{1,0:T(2,128)} %bitcast.17, ...), custom_call_target="tpu_custom_call" | custom-call | flops 60000000 | bytes 4000000 | tf_op jit(solution)/shard_map/pallas_call | solution.py:565
  30.4 0.8 %copy.10 = f32[2,72,8,128]{3,2,1,0:T(8,128)} copy(f32[2,72,8,128]{3,2,1,0:T(8,128)S(1)} %bitcast.11) | data formatting | bytes 1179648

commit v3 on v2

--- a/solution.py
+++ b/solution.py
@@ -9,7 +9,6 @@
 
 OLEV = 60
 CHUNK = 24
-RELAY = 2
 MESH = pl.DeviceIdType.MESH
 
 
@@ -63,7 +62,6 @@
     y0_send,
     y0_recv,
     here,
-    near,
     go,
 ):
     rows = lax.axis_size("comp")
@@ -100,21 +98,13 @@
         )
     ]
     get_fields, get_sends, get_tracers, get_vertical, get_lateral, get_recvs, get_gain = loads
-    for load in loads:
-        load.start()
+    get_fields.start()
+    get_sends.start()
 
     def get_weights(base, count):
         return pltpu.make_async_copy(
             weights.at[pl.ds(base, count)], wts.at[pl.ds(0, count)], load_sem.at[7]
         )
-
-    @pl.when(is_ocean)
-    def _():
-        get_weights(0, atmos).start()
-
-    @pl.when(is_atmos)
-    def _():
-        get_weights(atmos, ocean).start()
 
     barrier = pltpu.get_barrier_semaphore()
 
@@ -135,6 +125,67 @@
         @pl.when(has_upper)
         def _():
             greet(row + 1, tile)
+
+    half = tiles // 2
+    odd = lax.rem(tile, 2) == 1
+    even = lax.rem(tile, 2) == 0
+    inner_left = jnp.logical_and(tile != 0, tile != half)
+    inner_right = jnp.logical_and(tile != half - 1, tile != tiles - 1)
+    first_of_left = jnp.logical_or(tile == 0, jnp.logical_and(odd, inner_left))
+    first_of_right = jnp.logical_and(odd, inner_right)
+    second_of_left = jnp.logical_and(even, inner_left)
+    second_of_right = jnp.logical_or(tile == tiles - 1, jnp.logical_and(even, inner_right))
+    middle = jnp.logical_or(tile == half - 1, tile == half)
+    across = 2 * half - 1 - tile
+    share = max(ocean // 2, 1)
+    helper = lax.rem(row - atmos, share)
+    helps = jnp.logical_and(row < share, middle)
+
+    @pl.when(helps)
+    def _():
+        for turn in range(ocean // share):
+            greet(atmos + turn * share + row, across)
+
+    @pl.when(is_ocean)
+    def _():
+        @pl.when(first_of_left)
+        def _():
+            greet(row, left)
+
+        @pl.when(first_of_right)
+        def _():
+            greet(row, right)
+
+        @pl.when(has_upper)
+        def _():
+            greet(row + 1, tile)
+
+    def release():
+        def free(to_row, to_tile):
+            pl.semaphore_signal(go, inc=1, device_id=(to_row, to_tile), device_id_type=MESH)
+
+        @pl.when(second_of_right)
+        def _():
+            free(row, right)
+
+        @pl.when(second_of_left)
+        def _():
+            free(row, left)
+
+        @pl.when(has_lower)
+        def _():
+            free(row - 1, tile)
+
+    for load in (get_tracers, get_vertical, get_lateral, get_recvs, get_gain):
+        load.start()
+
+    @pl.when(is_ocean)
+    def _():
+        get_weights(0, atmos).start()
+
+    @pl.when(is_atmos)
+    def _():
+        get_weights(atmos, ocean).start()
 
     def list_blocks():
         get_fields.wait()
@@ -157,7 +208,7 @@
             src_ref=outgoing.at[place],
             dst_ref=incoming.at[row - own_base],
             send_sem=remap_send,
-            recv_sem=remap_recv,
+            recv_sem=remap_recv.at[row - own_base],
             device_id=(base + place, tile),
             device_id_type=MESH,
         ).start()
@@ -165,9 +216,22 @@
     @pl.when(is_ocean)
     def _():
         list_blocks()
-        pl.semaphore_wait(barrier, atmos)
-        pl.semaphore_signal(here, inc=1, device_id=(RELAY, tile), device_id_type=MESH)
+        pl.semaphore_wait(
+            barrier,
+            atmos
+            + second_of_left.astype(jnp.int32)
+            + second_of_right.astype(jnp.int32)
+            + has_lower.astype(jnp.int32)
+            + middle.astype(jnp.int32),
+        )
+
+        @pl.when(middle)
+        def _():
+            pl.semaphore_signal(here, inc=1, device_id=(helper, across), device_id_type=MESH)
+
         for place in range(atmos):
+            if place == atmos // 3:
+                release()
             fill(0, place)
             send_block(0, place, atmos)
 
@@ -297,14 +361,23 @@
 
     lax.fori_loop(0, chunks, pack_first, 0)
 
-    def await_blocks(count):
+    def await_blocks(place):
         pltpu.make_async_copy(
-            incoming.at[pl.ds(0, count)], incoming.at[pl.ds(0, count)], remap_recv
+            incoming.at[place], incoming.at[place], remap_recv.at[place]
         ).wait()
 
     @pl.when(is_ocean)
     def _():
-        pl.semaphore_wait(go, 1)
+        releases = (
+            first_of_left.astype(jnp.int32)
+            + first_of_right.astype(jnp.int32)
+            + has_upper.astype(jnp.int32)
+            + middle.astype(jnp.int32)
+        )
+
+        @pl.when(releases > 0)
+        def _():
+            pl.semaphore_wait(go, releases)
 
     def send_first(turn, carry):
         start_edges(0, chunks - 1 - turn)
@@ -382,75 +455,55 @@
     get_recvs.wait()
     get_gain.wait()
 
-    def remap(base, count):
-        def one(place, carry):
-            for slot in range(2):
-                lands = sub == recvs[slot, base + place]
-                column = pl.ds(pl.multiple_of((place * 2 + slot) * 128, 128), 128)
-                for pair in range(2):
-                    value = jnp.concatenate(
-                        [
-                            jnp.where(
-                                lands,
-                                jnp.broadcast_to(
-                                    incoming[place, slot * 4 + field : slot * 4 + field + 1, :],
-                                    (8, 128),
-                                ),
-                                0.0,
-                            )
-                            for field in (2 * pair, 2 * pair + 1)
-                        ],
-                        axis=0,
-                    )
-                    coarse = value.astype(jnp.bfloat16)
-                    fine = (value - coarse.astype(jnp.float32)).astype(jnp.bfloat16)
-                    spread[16 * pair : 16 * pair + 16, column] = coarse
-                    spread[32 + 16 * pair : 48 + 16 * pair, column] = fine
-            return carry
-
-        lax.fori_loop(0, count, one, 0, unroll=2)
-        get_weights(base, count).wait()
-        total = jnp.dot(
-            spread[:, : count * 256],
-            wts[:count].reshape(count * 256, 128),
+    def place_blocks(base, place):
+        await_blocks(place)
+        for slot in range(2):
+            lands = sub == recvs[slot, base + place]
+            column = pl.ds(pl.multiple_of((place * 2 + slot) * 128, 128), 128)
+            for pair in range(2):
+                value = jnp.concatenate(
+                    [
+                        jnp.where(
+                            lands,
+                            jnp.broadcast_to(
+                                incoming[place, slot * 4 + field : slot * 4 + field + 1, :],
+                                (8, 128),
+                            ),
+                            0.0,
+                        )
+                        for field in (2 * pair, 2 * pair + 1)
+                    ],
+                    axis=0,
+                )
+                coarse = value.astype(jnp.bfloat16)
+                fine = (value - coarse.astype(jnp.float32)).astype(jnp.bfloat16)
+                spread[16 * pair : 16 * pair + 16, column] = coarse
+                spread[32 + 16 * pair : 48 + 16 * pair, column] = fine
+
+    def product(start, count):
+        return jnp.dot(
+            spread[:, start * 256 : (start + count) * 256],
+            wts[start : start + count].reshape(count * 256, 128),
             preferred_element_type=jnp.float32,
         )
+
+    def force(total):
         remapped = total[:32] + total[32:]
-        low = high = jnp.zeros((8, 128), jnp.float32)
         values = []
         for var in range(2):
-            force = gains[var, 0] * remapped[:8]
+            value = gains[var, 0] * remapped[:8]
             for field in range(1, 4):
-                force = force + gains[var, field] * remapped[8 * field : 8 * field + 8]
-            forcing[var] = force
-            low, high = add_lanes(low, high, force, var)
-            values.append(force)
+                value = value + gains[var, field] * remapped[8 * field : 8 * field + 8]
+            forcing[var] = value
+            values.append(value)
+        x0_out[0] = jnp.where(sub == 0, values[0][7:8, :], values[1][7:8, :])
         x0_out[1] = jnp.where(sub == 0, values[0][0:1, :], values[1][0:1, :])
-        x0_out[0] = jnp.where(sub == 0, values[0][7:8, :], values[1][7:8, :])
-        put_y(y0_out, y0_in, low, high)
-
-    def force():
-        @pl.when(row == RELAY)
-        def _():
-            pl.semaphore_wait(here, ocean)
-            for side in (left, right):
-                pl.semaphore_signal(near, inc=1, device_id=(row, side), device_id_type=MESH)
-            pl.semaphore_wait(near, 2)
-            for partner in range(atmos, rows):
-                pl.semaphore_signal(go, inc=1, device_id=(partner, tile), device_id_type=MESH)
-
-        @pl.when(is_atmos)
-        def _():
-            await_blocks(ocean)
-            remap(atmos, ocean)
-
-        @pl.when(is_ocean)
-        def _():
-            await_blocks(atmos)
-            remap(0, atmos)
-
         copy_x0(0).start()
         copy_x0(1).start()
+        low = high = jnp.zeros((8, 128), jnp.float32)
+        for var in range(2):
+            low, high = add_lanes(low, high, values[var], var)
+        put_y(y0_out, y0_in, low, high)
 
         @pl.when(has_lower)
         def _():
@@ -460,11 +513,41 @@
         def _():
             copy_y0(0).start()
 
+    def exchange():
         @pl.when(is_atmos)
         def _():
+            get_weights(atmos, ocean).wait()
+            total = jnp.zeros((64, 128), jnp.float32)
+            part = max(ocean // 4, 1)
+            for start in range(0, ocean, part):
+                for place in range(start, start + part):
+                    place_blocks(atmos, place)
+                total = total + product(start, part)
+            force(total)
             for place in range(ocean):
                 send_block(atmos, place, 0)
 
+            @pl.when(helps)
+            def _():
+                pl.semaphore_wait(here, ocean // share)
+                for turn in range(ocean // share):
+                    pl.semaphore_signal(
+                        go,
+                        inc=1,
+                        device_id=(atmos + turn * share + row, tile),
+                        device_id_type=MESH,
+                    )
+
+        @pl.when(is_ocean)
+        def _():
+            def one(place, carry):
+                place_blocks(0, place)
+                return carry
+
+            lax.fori_loop(0, atmos, one, 0)
+            get_weights(0, atmos).wait()
+            force(product(0, atmos))
+
     forced_first = jnp.logical_and(row >= 2 * atmos // 3, is_atmos)
     steps_first = jnp.where(forced_first, 1, 0)
 
@@ -475,7 +558,7 @@
 
         @pl.when(turn != steps_first)
         def _():
-            force()
+            exchange()
 
         return carry
 
@@ -497,27 +580,11 @@
 
         lax.fori_loop(0, chunks, end, 0)
 
-    copy_x0(0).wait_recv()
-    copy_x0(1).wait_recv()
-
-    @pl.when(has_lower)
-    def _():
-        copy_y0(0).wait_recv()
-
-    @pl.when(has_upper)
-    def _():
-        copy_y0(1).wait_recv()
-
-    merged = merge(y0_in[0], y0_in[1])
+    lateral_here = lat[...].astype(jnp.float32)
     for var in range(2):
-        force = forcing[var]
-        x_low = jnp.broadcast_to(x0_in[0, var : var + 1, :], (8, 128))
-        x_high = jnp.broadcast_to(x0_in[1, var : var + 1, :], (8, 128))
-        mixing = rate[1] * force
-        effect = lat[...].astype(jnp.float32) * (
-            sides_of(force, x_low, x_high, merged, var) - 4.0 * force
-        )
-        out[tile_of(var * levels), :] += 2.0 * force + (effect - mixing)
+        value = forcing[var]
+        mixing = rate[1] * value
+        out[tile_of(var * levels), :] += 2.0 * value - mixing - 4.0 * lateral_here * value
         out[tile_of(var * levels + 1), :] += mixing
 
     copy_x0(0).wait_send()
@@ -526,10 +593,12 @@
     @pl.when(has_lower)
     def _():
         copy_y0(1).wait_send()
+        copy_y0(0).wait_recv()
 
     @pl.when(has_upper)
     def _():
         copy_y0(0).wait_send()
+        copy_y0(1).wait_recv()
 
     @pl.when(is_ocean)
     def _():
@@ -542,6 +611,16 @@
         pltpu.make_async_copy(
             outgoing.at[pl.ds(0, ocean)], outgoing.at[pl.ds(0, ocean)], remap_send
         ).wait()
+
+    merged = merge(y0_in[0], y0_in[1])
+    copy_x0(0).wait_recv()
+    copy_x0(1).wait_recv()
+    for var in range(2):
+        x_low = jnp.broadcast_to(x0_in[0, var : var + 1, :], (8, 128))
+        x_high = jnp.broadcast_to(x0_in[1, var : var + 1, :], (8, 128))
+        out[tile_of(var * levels), :] += lateral_here * sides_of(
+            forcing[var], x_low, x_high, merged, var
+        )
 
 
 def per_device(
@@ -593,7 +672,7 @@
             pltpu.VMEM((2, 8, 128), f32),
             dma((8,)),
             dma,
-            dma,
+            dma((atmos,)),
             dma((2, 2, chunks)),
             dma((2, 2, chunks)),
             dma((2, 2, chunks)),
@@ -602,7 +681,6 @@
             dma((2,)),
             dma((2,)),
             dma((2,)),
-            pltpu.SemaphoreType.REGULAR,
             pltpu.SemaphoreType.REGULAR,
             pltpu.SemaphoreType.REGULAR,
         ],

time: 31.5 us -> 30.3 us (0.962)
  the two profiles are of different devices: /device:TPU:768 before, /device:TPU:2 now
where the time goes in v3:
time: 30.3 us; the launch traced here: 30.1 us
  Pallas kernels  29.3 us (97%)
  local copies, waits for them, and re-layouts  0.82 us (3%)
    pallas_call x1, Pallas kernels, per_device(): pl.pallas_call(functools.partial(kernel, levels), out_shape=pltpu.VMEM((c...  29.3 us
    unnamed x1, local copies, waits for them, and re-layouts  0.82 us

profile of v3, /device:TPU:2, one launch (start us, length us, event | category | flops | bytes accessed | tf_op | source)
XLA Modules:
  0.0 30.1 jit_solution(1512990405382211250)
XLA Ops:
  0.0 29.3 %shard_map.82 = f32[1152,128]{1,0:T(8,128)S(1)} custom-call(f32[1152,128]{1,0:T(8,128)} %bitcast.13, f32[32,128]{1,0:T(8,128)} %bitcast.14, bf16[8,128]{1,0:T(8,128)(2,1)} %lateral.1, bf16[71,8,128]{2,1,0:T(8,128)(2,1)} %vertical.1, f32[2,4]{1,0:T(2,128)} %bitcast.15, s32[2,32]{1,0:T(2,128)} %bitcast.16, s32[2,32]{1,0:T(2,128)} %bitcast.17, ...), custom_call_target="tpu_custom_call" | custom-call | flops 60000000 | bytes 4000000 | tf_op jit(solution)/shard_map/pallas_call | solution.py:644
  29.3 0.8 %copy.10 = f32[2,72,8,128]{3,2,1,0:T(8,128)} copy(f32[2,72,8,128]{3,2,1,0:T(8,128)S(1)} %bitcast.11) | data formatting | bytes 1179648

commit v4 on v3

--- a/solution.py
+++ b/solution.py
@@ -87,9 +87,9 @@
         pltpu.make_async_copy(source, target, load_sem.at[place])
         for place, (source, target) in enumerate(
             [
-                (fields, surf),
+                (fields, surf.at[pl.ds(0, 32)]),
                 (send_slots, sends),
-                (tracers, first),
+                (tracers, first.at[pl.ds(0, 16 * levels)]),
                 (vertical, ver),
                 (lateral, lat),
                 (recv_slots, recvs),
@@ -647,12 +647,12 @@
         in_specs=[hbm] * 8,
         out_specs=pl.BlockSpec(memory_space=pltpu.VMEM),
         scratch_shapes=[
-            pltpu.VMEM((cells, 128), f32),
-            pltpu.VMEM((cells, 128), f32),
+            pltpu.VMEM((cells + 8, 128), f32),
+            pltpu.VMEM((cells + 8, 128), f32),
             pltpu.VMEM((8, 128), bf16),
             pltpu.VMEM((levels - 1, 8, 128), bf16),
             pltpu.VMEM((levels + 1, 8, 128), f32),
-            pltpu.VMEM((32, 128), f32),
+            pltpu.VMEM((40, 128), f32),
             pltpu.VMEM((9, 8, 128), f32),
             pltpu.VMEM((atmos, 8, 128), f32),
             pltpu.VMEM((atmos, 8, 128), f32),

time: 30.3 us -> 30.3 us (level)
  no operation moved by 1% of the time
where the time goes in v4:
time: 30.3 us; the launch traced here: 30.1 us
  Pallas kernels  29.3 us (97%)
  local copies, waits for them, and re-layouts  0.82 us (3%)
    pallas_call x1, Pallas kernels, per_device(): pl.pallas_call(functools.partial(kernel, levels), out_shape=pltpu.VMEM((c...  29.3 us
    unnamed x1, local copies, waits for them, and re-layouts  0.82 us

profile of v4, /device:TPU:2, one launch (start us, length us, event | category | flops | bytes accessed | tf_op | source)
XLA Modules:
  0.0 30.1 jit_solution(13871587724118171464)
XLA Ops:
  0.0 29.3 %shard_map.82 = f32[1152,128]{1,0:T(8,128)S(1)} custom-call(f32[1152,128]{1,0:T(8,128)} %bitcast.13, f32[32,128]{1,0:T(8,128)} %bitcast.14, bf16[8,128]{1,0:T(8,128)(2,1)} %lateral.1, bf16[71,8,128]{2,1,0:T(8,128)(2,1)} %vertical.1, f32[2,4]{1,0:T(2,128)} %bitcast.15, s32[2,32]{1,0:T(2,128)} %bitcast.16, s32[2,32]{1,0:T(2,128)} %bitcast.17, ...), custom_call_target="tpu_custom_call" | custom-call | flops 60000000 | bytes 4000000 | tf_op jit(solution)/shard_map/pallas_call | solution.py:644
  29.3 0.8 %copy.10 = f32[2,72,8,128]{3,2,1,0:T(8,128)} copy(f32[2,72,8,128]{3,2,1,0:T(8,128)S(1)} %bitcast.11) | data formatting | bytes 1179648

commit v5 on v4

--- a/solution.py
+++ b/solution.py
@@ -229,11 +229,18 @@
         def _():
             pl.semaphore_signal(here, inc=1, device_id=(helper, across), device_id_type=MESH)
 
-        for place in range(atmos):
-            if place == atmos // 3:
-                release()
+        def one(turn, carry):
+            step = lax.rem(turn, share)
+            run = turn // share
+            run = jnp.where(lax.rem(run, 2) == 0, run // 2, atmos // share - 1 - run // 2)
+            place = run * share + jnp.where(2 * helper < share, share - 1 - step, step)
             fill(0, place)
             send_block(0, place, atmos)
+            return carry
+
+        lax.fori_loop(0, atmos // 3, one, 0)
+        release()
+        lax.fori_loop(atmos // 3, atmos, one, 0)
 
     @pl.when(is_atmos)
     def _():

time: 30.3 us -> 30.4 us (level)
  no operation moved by 1% of the time
where the time goes in v5:
time: 30.4 us; the launch traced here: 30.2 us
  Pallas kernels  29.4 us (97%)
  local copies, waits for them, and re-layouts  0.82 us (3%)
    pallas_call x1, Pallas kernels, per_device(): pl.pallas_call(functools.partial(kernel, levels), out_shape=pltpu.VMEM((c...  29.4 us
    unnamed x1, local copies, waits for them, and re-layouts  0.82 us

profile of v5, /device:TPU:2, one launch (start us, length us, event | category | flops | bytes accessed | tf_op | source)
XLA Modules:
  0.0 30.2 jit_solution(1280847766980051494)
XLA Ops:
  0.0 29.4 %shard_map.82 = f32[1152,128]{1,0:T(8,128)S(1)} custom-call(f32[1152,128]{1,0:T(8,128)} %bitcast.13, f32[32,128]{1,0:T(8,128)} %bitcast.14, bf16[8,128]{1,0:T(8,128)(2,1)} %lateral.1, bf16[71,8,128]{2,1,0:T(8,128)(2,1)} %vertical.1, f32[2,4]{1,0:T(2,128)} %bitcast.15, s32[2,32]{1,0:T(2,128)} %bitcast.16, s32[2,32]{1,0:T(2,128)} %bitcast.17, ...), custom_call_target="tpu_custom_call" | custom-call | flops 60000000 | bytes 4000000 | tf_op jit(solution)/shard_map/pallas_call | solution.py:651
  29.4 0.8 %copy.10 = f32[2,72,8,128]{3,2,1,0:T(8,128)} copy(f32[2,72,8,128]{3,2,1,0:T(8,128)S(1)} %bitcast.11) | data formatting | bytes 1179648
